TPU v7x, 768 devices: a whole 4x8x12 slice. The times are simulated.
768 devices in a mesh: row: 24 (over z, core), col: 32 (over y, x).
Axes of the slice: x: 4, y: 8, z: 12, core: 2. Of those that a mesh axis runs over, the one named last changes fastest.
Arguments:
- three_center: bfloat16 [24, 384, 131072], P(None, 'row', 'col'), may hold values from -0.0625 to 0.0625
- density: bfloat16 [131072, 1024], P('col'), may hold values from -6 to 6
- pair_mask: int32 [384, 1024], P('row', 'col'), may hold values from 0 to 1, as said below
- metric: float32 [24, 24], replicated, may hold values from -1.25 to 1.25
- aux_pairs: float32 [24, 1024, 1024], P('row', 'col'), may hold values from -0.0390625 to 0.0390625
Outputs:
- exchange_part: float32 [384, 1024], P('row')
Inputs may be any that keep to these rules, and one draw needn't show every extreme that they name: `pair_mask`: in each row mu the ones form one run of consecutive atom blocks, which may start anywhere.
All inputs are finite; a program needn't handle non-finite values.
Results may differ from a plain program's by a relative error of at most 0.0003.
Values sent between devices are 32-bit elements; how exact they have to be, the bound alone decides.
No kernel may reach another device: no remote copies, remote signals or barrier semaphores. Data moves between devices by JAX's collectives and lax.ppermute only.
A program may use at most 64 MiB of HBM per device.

v0:
```python
import jax
import jax.numpy as jnp
from jax import lax
from jax.sharding import PartitionSpec as P

BLK = 128


def on_device(three_center, density, pair_mask, metric, aux_pairs):
    expand = jnp.repeat(pair_mask, BLK, axis=1).astype(jnp.bfloat16)
    masked = three_center * expand[None]
    coeffs = lax.psum_scatter(
        jnp.einsum("ns,pmn->spm", density, masked, preferred_element_type=jnp.float32),
        "col",
        scatter_dimension=0,
        tiled=True,
    )
    fitted = jnp.einsum("qp,spm->sqm", metric, coeffs, precision=lax.Precision.HIGHEST)
    regrouped = lax.all_to_all(fitted, "row", split_axis=1, concat_axis=2, tiled=True)
    summed = jnp.einsum("sqm,qsl->ml", regrouped, aux_pairs, precision=lax.Precision.HIGHEST)
    rowpart = lax.psum_scatter(summed, "row", scatter_dimension=0, tiled=True)
    return lax.psum(rowpart, "col")


def solution(mesh):
    placed = (P(None, "row", "col"), P("col", None), P("row", "col"), P(), P("row", "col", None))
    return jax.shard_map(
        on_device, mesh=mesh, in_specs=placed, out_specs=P("row", None), check_vma=False
    )
```

profile of v0, /device:TPU:12, one launch (start us, length us, event | category | flops | bytes accessed | tf_op | source)
XLA Modules:
  0.0 540.7 jit_solution(15695041874200637258)
XLA Ops:
  6.5 0.0 copy-start
  6.5 0.0 reduce-scatter.7.cloned.1.call-start
  6.5 0.7 convert_element_type.11
  7.3 0.1 broadcast_in_dim.4
  7.4 0.1 copy.20
  7.5 2.1 broadcast_multiply_fusion
  9.6 7.5 %fusion.3 = f32[1024,24,16]{0,1,2:T(8,128)S(1)} fusion(bf16[4096,1024]{1,0:T(8,128)(2,1)} %param.6, bf16[24,16,4096]{2,1,0:T(8,128)(2,1)S(1)} %broadcast_multiply_fusion), kind=kOutput, calls=%fused_computation.4 | convolution fusion | flops 3221225472 | bytes 13107200 | tf_op jit(solution)/shard_map/ns,pmn->spm/dot_general | solution.py:13
  17.1 6.2 %copy.9 = f32[1024,24,16]{1,2,0:T(8,128)} copy(f32[1024,24,16]{0,1,2:T(8,128)S(1)} %fusion.3) | data formatting | bytes 3145728
  23.3 0.0 copy-start.1
  23.3 7.6 %reshape.21 = f32[1024,384]{1,0:T(8,128)} reshape(f32[1024,16,24]{2,1,0:T(8,128)} %bitcast.28) | data formatting | bytes 3145728
  30.9 0.0 reduce-scatter.7.cloned.1.call-update
  30.9 0.0 reduce-scatter.5.cloned.1.call-start
  31.0 232.1 %reduce-scatter.7.cloned.1.call-done = f32[32,384]{1,0:T(8,128)} async-done(((f32[1024,384]{1,0:T(8,128)}), f32[32,384]{1,0:T(8,128)}) %reduce-scatter.7.cloned.1.call-update) | async-done | bytes 49168
  263.1 1.0 reshape.22
  264.1 0.0 copy-done.1
  264.1 1.1 convolution_bitcast_fusion
  265.3 0.1 reshape.23
  265.4 20.6 %all_to_all.4 = f32[24,1,512]{2,1,0:T(1,128)S(1)} all-to-all(f32[24,1,512]{2,1,0:T(1,128)S(1)} %reshape.23), channel_id=1, replica_groups=mesh['row'=24,'col'=32] {'row'}, dimensions={0} | all-to-all | bytes 98304 | tf_op jit(solution)/shard_map/all_to_all | solution.py:19
  286.0 0.5 broadcast.1
  286.5 0.8 reduce
  287.3 0.1 reshape.24
  287.4 0.0 copy-done
  287.4 2.5 fusion.9
  289.9 0.0 reduce-scatter.5.cloned.1.call-update
  290.0 0.0 all-reduce.2.cloned.1.call-start
  290.0 80.4 %reduce-scatter.5.cloned.1.call-done = f32[16,1024]{1,0:T(8,128)} async-done(((f32[384,1024]{1,0:T(8,128)}), f32[16,1024]{1,0:T(8,128)}) %reduce-scatter.5.cloned.1.call-update) | async-done | bytes 65552 | tf_op jit(solution)/shard_map/reduce_scatter | solution.py:21
  370.4 0.0 all-reduce.2.cloned.1.call-update
  370.5 162.2 %all-reduce.2.cloned.1.call-done = f32[16,1024]{1,0:T(8,128)} async-done(((f32[16,1024]{1,0:T(8,128)}), f32[16,1024]{1,0:T(8,128)}) %all-reduce.2.cloned.1.call-update) | async-done | bytes 65552 | tf_op jit(solution)/shard_map/psum | solution.py:22
  532.7 1.5 copy.23
  (1 shorter events, 0.0 us)
Async XLA Ops:
  6.5 280.9 %copy-start = (f32[1,32,1024]{2,1,0:T(8,128)S(1)}, f32[1,32,1024]{2,1,0:T(8,128)}, u32[]{:S(2)}) copy-start(f32[1,32,1024]{2,1,0:T(8,128)} %param.9) | copy-start | bytes 393220
  6.5 256.6 %reduce-scatter.7.cloned.1.call-start = ((), (), s32[]{:S(2)}) async-start(), calls=%async_computation.5 | async-start | bytes 1622016
  23.3 240.8 %copy-start.1 = (f32[24,24]{1,0:T(8,128)S(1)}, f32[24,24]{1,0:T(8,128)}, u32[]{:S(2)}) copy-start(f32[24,24]{1,0:T(8,128)} %param.8) | copy-start | bytes 6916
  30.9 339.5 %reduce-scatter.5.cloned.1.call-start = ((), (), s32[]{:S(2)}) async-start(), calls=%async_computation.3 | async-start | bytes 1638400 | tf_op jit(solution)/shard_map/reduce_scatter | solution.py:21
  290.0 242.7 %all-reduce.2.cloned.1.call-start = ((), (), s32[]{:S(2)}) async-start(), calls=%async_computation.4 | async-start | bytes 131072 | tf_op jit(solution)/shard_map/psum | solution.py:22
Sparse Core Ops, SparseCore 0:
  31.0 232.0 reduce-scatter.6
  290.1 80.3 reduce-scatter.4
  374.3 158.3 all-reduce.1
where the time goes:
time: 541 us
  waiting for transfers between devices  475 us (88%)
  blocking collectives  20.6 us (4%)
  local copies, waits for them, and re-layouts  17.2 us (3%)
  between operations  13.2 us (2%)
  matrix products  11.2 us (2%)
    unnamed x4, waiting for transfers between devices  232 us
    psum x1, waiting for transfers between devices, on_device(): return lax.psum(rowpart, 'col')  162 us
    reduce_scatter x1, waiting for transfers between devices, on_device(): rowpart = lax.psum_scatter(summed, 'row', scatter_dimension=0, tiled=True)  80.4 us
    all_to_all x1, blocking collectives, on_device(): lax.all_to_all(fitted, 'row', split_axis=1, concat_axis=2, tiled=True)  20.6 us
    unnamed x11, local copies, waits for them, and re-layouts  16.5 us
  transfers between devices with their start and end apart: 3, of which 3 were waited for; matrix products, arithmetic and copies ran while one was open for 0% of the time, Pallas kernels for 0%

commit v1 on v0

v1 whole, which is shorter than its diff:
```python
import functools

import jax
import jax.numpy as jnp
from jax import lax
from jax.experimental import pallas as pl
from jax.experimental.pallas import tpu as pltpu
from jax.sharding import Mesh
from jax.sharding import PartitionSpec as P

BLK = 128
NZ, NCORE, NY, NX = 12, 2, 8, 4
NP, MU, NLOC, L = 24, 16, 4096, 1024
SIG = 32
ROWS = NP * MU
KB = 512
F32, BF16 = jnp.float32, jnp.bfloat16


def coeff_kernel(mask_ref, three_ref, dens_ref, out_ref, acc, wide):
    step = pl.program_id(0)

    @pl.when(step == 0)
    def _():
        mask = mask_ref[...].astype(F32)
        per = KB // BLK
        for b in range(NLOC // BLK):
            col = jnp.broadcast_to(mask[:, b : b + 1], (MU, BLK)).astype(BF16)
            wide[b // per, :, (b % per) * BLK : (b % per + 1) * BLK] = col

    masked = three_ref[...] * wide[step][None]
    part = jnp.dot(masked.reshape(ROWS, KB), dens_ref[...], preferred_element_type=F32)

    @pl.when(step == 0)
    def _():
        acc[...] = part

    @pl.when(step > 0)
    def _():
        acc[...] += part

    @pl.when(step == pl.num_programs(0) - 1)
    def _():
        for y in range(NY):
            turned = acc[:, y * BLK : (y + 1) * BLK].T
            for x in range(NX):
                out_ref[x, y * SIG : (y + 1) * SIG, :] = turned[x * SIG : (x + 1) * SIG]


def partial_coeffs(pair_mask, three_center, density):
    steps = NLOC // KB
    return pl.pallas_call(
        coeff_kernel,
        grid=(steps,),
        in_specs=[
            pl.BlockSpec((MU, NLOC // BLK), lambda i: (0, 0)),
            pl.BlockSpec((NP, MU, KB), lambda i: (0, 0, i)),
            pl.BlockSpec((KB, L), lambda i: (i, 0)),
        ],
        out_specs=pl.BlockSpec((NX, NY * SIG, ROWS), lambda i: (0, 0, 0)),
        out_shape=jax.ShapeDtypeStruct((NX, NY * SIG, ROWS), F32),
        scratch_shapes=[pltpu.VMEM((ROWS, L), F32), pltpu.VMEM((steps, MU, KB), BF16)],
        compiler_params=pltpu.CompilerParams(vmem_limit_bytes=58 * 1024 * 1024),
        cost_estimate=pl.CostEstimate(
            flops=2 * ROWS * NLOC * L, bytes_accessed=13_000_000, transcendentals=0
        ),
    )(pair_mask, three_center, density)


def halves(a):
    top = a.astype(BF16)
    return top, (a - top.astype(F32)).astype(BF16)


def dot3(a, b):
    a_top, a_low = halves(a)
    b_top, b_low = halves(b)
    dot = functools.partial(jnp.dot, preferred_element_type=F32)
    return dot(a_top, b_top) + (dot(a_low, b_top) + dot(a_top, b_low))


def exchange_kernel(parts_ref, mix_ref, *refs):
    aux_refs, out_ref = refs[:-1], refs[-1]
    coeffs = parts_ref[0]
    for y in range(1, NY):
        coeffs = coeffs + parts_ref[y]
    fitted = dot3(coeffs, mix_ref[...]).T
    total = None
    slots = NP // len(aux_refs)
    for g, aux_ref in enumerate(aux_refs):
        left = jnp.concatenate(
            [
                fitted[(g * slots + s) * MU : (g * slots + s + 1) * MU]
                for s in range(slots)
            ],
            axis=1,
        )
        term = dot3(left, aux_ref[...])
        total = term if total is None else total + term
    for c in range(NY * NX):
        lane, row = (c // 4) * BLK, (c % 4) * 4
        out_ref[c] = total[row : row + 4, lane : lane + BLK]


def exchange_partial(parts, mix, aux_groups):
    n = 2 + len(aux_groups)
    return pl.pallas_call(
        exchange_kernel,
        in_specs=[pl.BlockSpec(memory_space=pltpu.VMEM)] * n,
        out_specs=pl.BlockSpec(memory_space=pltpu.VMEM),
        out_shape=jax.ShapeDtypeStruct((NY * NX, 4, BLK), F32),
        compiler_params=pltpu.CompilerParams(vmem_limit_bytes=32 * 1024 * 1024),
        cost_estimate=pl.CostEstimate(
            flops=6 * MU * NP * SIG * L, bytes_accessed=4_000_000, transcendentals=0
        ),
    )(parts, mix, *aux_groups)


def shift(a, axis, size, by):
    return lax.ppermute(a, axis, [(i, (i + by) % size) for i in range(size)])


def on_device(three_center, density, pair_mask, metric, aux_pairs):
    z, core = lax.axis_index("z"), lax.axis_index("core")

    part = partial_coeffs(pair_mask, three_center, density)

    own = aux_pairs.reshape(SIG, L)
    far = jnp.concatenate(
        [own] + [shift(own, "z", NZ, by) for by in (3, 9, 6)], axis=0
    )
    groups = [far, shift(far, "z", NZ, 1), shift(far, "z", NZ, NZ - 1)]
    groups = groups + [shift(g, "core", NCORE, 1) for g in groups]
    away = jnp.array([0, -3, 3, 6], jnp.int32)
    origin = jnp.concatenate([away, away - 1, away + 1]) + z
    origin = lax.rem(origin + 2 * NZ, NZ) * NCORE
    slots = jnp.concatenate([origin + core, origin + (1 - core)])
    chosen = jnp.take(metric, slots, axis=0)
    mix = chosen.T[:, None, :, None] * jnp.eye(MU, dtype=F32)[None, :, None, :]
    mix = mix.reshape(ROWS, ROWS)

    got = lax.all_to_all(part, "x", 0, 0, tiled=True)
    mine = jnp.sum(got, axis=0).reshape(NY, SIG, ROWS)
    got = lax.all_to_all(mine, "y", 0, 0, tiled=True)
    term = exchange_partial(got, mix, groups)
    got = lax.all_to_all(term, ("y", "x"), 0, 0, tiled=True)
    done = jnp.broadcast_to(jnp.sum(got, axis=0)[None], (NY * NX, 4, BLK))
    full = lax.all_to_all(done, ("y", "x"), 0, 0, tiled=True)
    return full.reshape(8, MU, BLK).transpose(1, 0, 2).reshape(MU, L)


def solution(mesh):
    grid = Mesh(mesh.devices.reshape(NZ, NCORE, NY, NX), ("z", "core", "y", "x"))
    row, col = ("z", "core"), ("y", "x")
    placed = (P(None, row, col), P(col, None), P(row, col), P(), P(row, col, None))
    return jax.shard_map(
        on_device, mesh=grid, in_specs=placed, out_specs=P(row, None), check_vma=False
    )
```

time: 541 us -> 114 us (0.21)
  the two profiles are of different devices: /device:TPU:12 before, /device:TPU:8 now
where the time goes in v1:
time: 114 us; the launch traced here: 113 us
  starting transfers between devices  47.9 us (42%)
  blocking collectives  32 us (28%)
  Pallas kernels  13.7 us (12%)
  waiting for transfers between devices  10.9 us (10%)
  local copies, waits for them, and re-layouts  4.88 us (4%)
  other arithmetic  3.73 us (3%)
    ppermute x8, starting transfers between devices, shift(): return lax.ppermute(a, axis, [(i, (i + by) % size) for i in range(size)])  36.1 us
    all_to_all x1, blocking collectives, on_device(): got = lax.all_to_all(term, ('y', 'x'), 0, 0, tiled=True)  19 us
    all_to_all x1, blocking collectives, on_device(): full = lax.all_to_all(done, ('y', 'x'), 0, 0, tiled=True)  13 us
    pallas_call x1, Pallas kernels, partial_coeffs(): pl.pallas_call(coeff_kernel, grid=(steps,), in_specs=[pl.BlockSpec((MU, N...  11.1 us
    ppermute x8, waiting for transfers between devices, shift(): return lax.ppermute(a, axis, [(i, (i + by) % size) for i in range(size)])  10.9 us
    all_to_all x1, starting transfers between devices, on_device(): got = lax.all_to_all(mine, 'y', 0, 0, tiled=True)  7.54 us
    all_to_all x1, starting transfers between devices, on_device(): got = lax.all_to_all(part, 'x', 0, 0, tiled=True)  4.29 us
    mul x1, local copies, waits for them, and re-layouts, on_device(): mix = chosen.T[:, None, :, None] * jnp.eye(MU, dtype=F32)[None, :, None, :]  3.58 us
  transfers between devices with their start and end apart: 10, of which 1 were waited for; matrix products, arithmetic and copies ran while one was open for 7% of the time, Pallas kernels for 0%

profile of v1, /device:TPU:8, one launch (start us, length us, event | category | flops | bytes accessed | tf_op | source)
XLA Modules:
  0.0 113.3 jit_solution(16088268339749118854)
XLA Ops:
  0.0 11.1 %shard_map.64 = f32[4,256,384]{2,1,0:T(8,128)} custom-call(s32[16,32]{1,0:T(8,128)} %mask_ref.1, bf16[24,16,4096]{2,1,0:T(8,128)(2,1)} %three_ref.1, bf16[4096,1024]{1,0:T(8,128)(2,1)} %dens_ref.1), custom_call_target="tpu_custom_call" | custom-call | flops 3221225472 | bytes 13000000 | tf_op jit(solution)/shard_map/pallas_call | solution.py:52
  11.2 4.3 %all-to-all-start = ((f32[4,256,384]{2,1,0:T(8,128)}), f32[4,256,384]{2,1,0:T(8,128)S(1)}, u32[]{:S(2)}, u32[]{:S(2)}) async-start(f32[4,256,384]{2,1,0:T(8,128)} %shard_map.64), calls=%async_computation | async-start | bytes 3145728 | tf_op jit(solution)/shard_map/all_to_all | solution.py:142
  15.5 15.1 %collective-permute-start.2 = (f32[32,1024]{1,0:T(8,128)S(1)}, f32[32,1024]{1,0:T(8,128)S(1)}, u32[]{:S(2)}, u32[]{:S(2)}) collective-permute-start(f32[32,1024]{1,0:T(8,128)S(1)} %bitcast.18), channel_id=1, source_target_pairs={{0,384},{64,448},{128,512},{192,576},{256,640},{320,704},{384,0},{... | collective-permute-start | bytes 393224 | tf_op jit(solution)/shard_map/ppermute | solution.py:120
  30.6 1.9 %collective-permute-start.1 = (f32[32,1024]{1,0:T(8,128)S(1)}, f32[32,1024]{1,0:T(8,128)S(1)}, u32[]{:S(2)}, u32[]{:S(2)}) collective-permute-start(f32[32,1024]{1,0:T(8,128)S(1)} %bitcast.19), channel_id=1, source_target_pairs={{0,576},{64,640},{128,704},{192,0},{256,64},{320,128},{384,192},{4... | collective-permute-start | bytes 393224 | tf_op jit(solution)/shard_map/ppermute | solution.py:120
  32.5 5.7 %collective-permute-start = (f32[32,1024]{1,0:T(8,128)S(1)}, f32[32,1024]{1,0:T(8,128)S(1)}, u32[]{:S(2)}, u32[]{:S(2)}) collective-permute-start(f32[32,1024]{1,0:T(8,128)S(1)} %bitcast.20), channel_id=1, source_target_pairs={{0,192},{64,256},{128,320},{192,384},{256,448},{320,512},{384,576}... | collective-permute-start | bytes 393224 | tf_op jit(solution)/shard_map/ppermute | solution.py:120
  38.3 0.0 collective-permute-done.2
  38.3 10.9 %collective-permute-done.1 = f32[32,1024]{1,0:T(8,128)S(1)} collective-permute-done((f32[32,1024]{1,0:T(8,128)S(1)}, f32[32,1024]{1,0:T(8,128)S(1)}, u32[]{:S(2)}, u32[]{:S(2)}) %collective-permute-start.1) | collective-permute-done | bytes 131104 | tf_op jit(solution)/shard_map/ppermute | solution.py:120
  49.1 0.0 collective-permute-done
  49.2 1.9 %collective-permute-start.3 = (f32[128,1024]{1,0:T(8,128)S(1)}, f32[128,1024]{1,0:T(8,128)S(1)}, u32[]{:S(2)}, u32[]{:S(2)}) collective-permute-start(f32[128,1024]{1,0:T(8,128)S(1)} %pad_maximum_fusion.refs_0_), channel_id=1, source_target_pairs={{0,64},{64,128},{128,192},{192,256},{256,320},{320,384},{384,448},... | collective-permute-start | bytes 1572872 | tf_op jit(solution)/shard_map/ppermute | solution.py:120
  51.1 5.1 %collective-permute-start.4 = (f32[128,1024]{1,0:T(8,128)S(1)}, f32[128,1024]{1,0:T(8,128)S(1)}, u32[]{:S(2)}, u32[]{:S(2)}) collective-permute-start(f32[128,1024]{1,0:T(8,128)S(1)} %pad_maximum_fusion.refs_0_), channel_id=1, source_target_pairs={{0,704},{64,0},{128,64},{192,128},{256,192},{320,256},{384,320},{4... | collective-permute-start | bytes 1572872 | tf_op jit(solution)/shard_map/ppermute | solution.py:120
  56.3 0.1 fusion.1
  56.4 0.0 all-to-all-done
  56.4 0.9 reduce_sum.18
  57.2 7.5 %all-to-all-start.1 = ((f32[8,32,384]{2,1,0:T(8,128)}), f32[8,32,384]{2,1,0:T(8,128)S(1)}, u32[]{:S(2)}, u32[]{:S(2)}) async-start(f32[8,32,384]{2,1,0:T(8,128)} %bitcast), calls=%async_computation.1 | async-start | bytes 786432 | tf_op jit(solution)/shard_map/all_to_all | solution.py:144
  64.8 0.1 compare_and_fusion
  64.9 0.6 gather_fusion
  65.4 1.9 %collective-permute-start.5 = (f32[128,1024]{1,0:T(8,128)S(1)}, f32[128,1024]{1,0:T(8,128)S(1)}, u32[]{:S(2)}, u32[]{:S(2)}) collective-permute-start(f32[128,1024]{1,0:T(8,128)S(1)} %pad_maximum_fusion.refs_0_), channel_id=1, source_target_pairs={{0,32},{32,0},{1,33},{33,1},{2,34},{34,2},{3,35},{35,3},{4,36},{36... | collective-permute-start | bytes 1572872 | tf_op jit(solution)/shard_map/ppermute | solution.py:120
  67.4 0.0 collective-permute-done.3.refs_1_
  67.4 2.4 %collective-permute-start.6 = (f32[128,1024]{1,0:T(8,128)S(1)}, f32[128,1024]{1,0:T(8,128)}, u32[]{:S(2)}, u32[]{:S(2)}) collective-permute-start(f32[128,1024]{1,0:T(8,128)S(1)} %collective-permute-done.3.refs_1_), channel_id=1, source_target_pairs={{0,32},{32,0},{1,33},{33,1},{2,34},{34,2},{3,35},{35,3},{4,36},{36... | collective-permute-start | bytes 1572872 | tf_op jit(solution)/shard_map/ppermute | solution.py:120
  69.8 0.0 collective-permute-done.4.refs_2_
  69.8 1.9 %collective-permute-start.7 = (f32[128,1024]{1,0:T(8,128)S(1)}, f32[128,1024]{1,0:T(8,128)}, u32[]{:S(2)}, u32[]{:S(2)}) collective-permute-start(f32[128,1024]{1,0:T(8,128)S(1)} %collective-permute-done.4.refs_2_), channel_id=1, source_target_pairs={{0,32},{32,0},{1,33},{33,1},{2,34},{34,2},{3,35},{35,3},{4,36},{36... | collective-permute-start | bytes 1572872 | tf_op jit(solution)/shard_map/ppermute | solution.py:120
  71.7 0.1 select_bitcast_fusion
  71.8 0.1 copy.9
  71.9 2.5 %broadcast_multiply_fusion = f32[24,16,24,16]{3,2,1,0:T(8,128)} fusion(f32[16,16]{1,0:T(8,128)S(1)} %fusion, f32[24,24]{1,0:T(8,128)S(1)} %copy.9), kind=kLoop, calls=%fused_computation.1 | loop fusion | flops 147456 | bytes 593152 | tf_op jit(solution)/shard_map/mul | solution.py:139
  74.4 3.6 %mul.48.mix_ref = f32[384,384]{1,0:T(8,128)S(1)} reshape(f32[24,16,24,16]{3,2,1,0:T(8,128)} %broadcast_multiply_fusion) | data formatting | bytes 1179648 | tf_op jit(solution)/shard_map/mul | solution.py:139
  78.0 0.0 collective-permute-done.5.refs_3_
  78.0 0.0 collective-permute-done.6.refs_4_
  78.0 0.0 all-to-all-done.1.parts_ref
  78.0 2.6 %shard_map.65 = f32[32,4,128]{2,1,0:T(4,128)S(1)} custom-call(f32[8,32,384]{2,1,0:T(8,128)S(1)} %all-to-all-done.1.parts_ref, f32[384,384]{1,0:T(8,128)S(1)} %mul.48.mix_ref, f32[128,1024]{1,0:T(8,128)S(1)} %pad_maximum_fusion.refs_0_, f32[128,1024]{1,0:T(8,128)S(1)} %collective-permute-done.3.refs_1_, f32[128,1024]{1,0:T(8,128)S(1)} %collective-permute-done.4.refs_2_, ...), custom_call_target="tpu_custom_call" | custom-call | flops 75497472 | bytes 4000000 | tf_op jit(solution)/shard_map/pallas_call | solution.py:107
  80.6 19.0 %all_to_all.20 = f32[32,4,128]{2,1,0:T(4,128)S(1)} all-to-all(f32[32,4,128]{2,1,0:T(4,128)S(1)} %shard_map.65), channel_id=1, replica_groups=mesh['z'=12,'core'=2,'y'=8,'x'=4] {'y','x'}, dimensions={0} | all-to-all | bytes 131072 | tf_op jit(solution)/shard_map/all_to_all | solution.py:146
  99.6 13.0 %all_to_all.21 = f32[32,4,128]{2,1,0:T(4,128)S(1)} all-to-all(f32[32,4,128]{2,1,0:T(4,128)S(1)} %broadcast_in_dim.20), channel_id=1, replica_groups=mesh['z'=12,'core'=2,'y'=8,'x'=4] {'y','x'}, dimensions={0} | all-to-all | bytes 131072 | tf_op jit(solution)/shard_map/all_to_all | solution.py:148
  112.7 0.6 copy.13
  (13 shorter events, 0.1 us)
Async XLA Ops:
  0.0 64.9 %copy-start = (f32[24,24]{1,0:T(8,128)S(1)}, f32[24,24]{1,0:T(8,128)}, u32[]{:S(2)}) copy-start(f32[24,24]{1,0:T(8,128)} %param.9) | copy-start | bytes 6916
  0.0 56.3 %copy-start.2 = (s32[12]{0:T(128)S(1)}, s32[12]{0:T(128)}, u32[]{:S(2)}) copy-start(s32[12]{0:T(128)} %constant.47) | copy-start | bytes 148
  0.0 15.4 %copy-start.1 = (f32[1,32,1024]{2,1,0:T(8,128)S(1)}, f32[1,32,1024]{2,1,0:T(8,128)}, u32[]{:S(2)}) copy-start(f32[1,32,1024]{2,1,0:T(8,128)} %param.10) | copy-start | bytes 393220
  11.2 45.2 %all-to-all-start = ((f32[4,256,384]{2,1,0:T(8,128)}), f32[4,256,384]{2,1,0:T(8,128)S(1)}, u32[]{:S(2)}, u32[]{:S(2)}) async-start(f32[4,256,384]{2,1,0:T(8,128)} %shard_map.64), calls=%async_computation | async-start | bytes 3145728 | tf_op jit(solution)/shard_map/all_to_all | solution.py:142
  15.5 22.8 %collective-permute-start.2 = (f32[32,1024]{1,0:T(8,128)S(1)}, f32[32,1024]{1,0:T(8,128)S(1)}, u32[]{:S(2)}, u32[]{:S(2)}) collective-permute-start(f32[32,1024]{1,0:T(8,128)S(1)} %bitcast.18), channel_id=1, source_target_pairs={{0,384},{64,448},{128,512},{192,576},{256,640},{320,704},{384,0},{... | collective-permute-start | bytes 393224 | tf_op jit(solution)/shard_map/ppermute | solution.py:120
  30.6 18.5 %collective-permute-start.1 = (f32[32,1024]{1,0:T(8,128)S(1)}, f32[32,1024]{1,0:T(8,128)S(1)}, u32[]{:S(2)}, u32[]{:S(2)}) collective-permute-start(f32[32,1024]{1,0:T(8,128)S(1)} %bitcast.19), channel_id=1, source_target_pairs={{0,576},{64,640},{128,704},{192,0},{256,64},{320,128},{384,192},{4... | collective-permute-start | bytes 393224 | tf_op jit(solution)/shard_map/ppermute | solution.py:120
  32.5 16.6 %collective-permute-start = (f32[32,1024]{1,0:T(8,128)S(1)}, f32[32,1024]{1,0:T(8,128)S(1)}, u32[]{:S(2)}, u32[]{:S(2)}) collective-permute-start(f32[32,1024]{1,0:T(8,128)S(1)} %bitcast.20), channel_id=1, source_target_pairs={{0,192},{64,256},{128,320},{192,384},{256,448},{320,512},{384,576}... | collective-permute-start | bytes 393224 | tf_op jit(solution)/shard_map/ppermute | solution.py:120
  49.2 18.2 %collective-permute-start.3 = (f32[128,1024]{1,0:T(8,128)S(1)}, f32[128,1024]{1,0:T(8,128)S(1)}, u32[]{:S(2)}, u32[]{:S(2)}) collective-permute-start(f32[128,1024]{1,0:T(8,128)S(1)} %pad_maximum_fusion.refs_0_), channel_id=1, source_target_pairs={{0,64},{64,128},{128,192},{192,256},{256,320},{320,384},{384,448},... | collective-permute-start | bytes 1572872 | tf_op jit(solution)/shard_map/ppermute | solution.py:120
  51.1 18.7 %collective-permute-start.4 = (f32[128,1024]{1,0:T(8,128)S(1)}, f32[128,1024]{1,0:T(8,128)S(1)}, u32[]{:S(2)}, u32[]{:S(2)}) collective-permute-start(f32[128,1024]{1,0:T(8,128)S(1)} %pad_maximum_fusion.refs_0_), channel_id=1, source_target_pairs={{0,704},{64,0},{128,64},{192,128},{256,192},{320,256},{384,320},{4... | collective-permute-start | bytes 1572872 | tf_op jit(solution)/shard_map/ppermute | solution.py:120
  57.2 20.8 %all-to-all-start.1 = ((f32[8,32,384]{2,1,0:T(8,128)}), f32[8,32,384]{2,1,0:T(8,128)S(1)}, u32[]{:S(2)}, u32[]{:S(2)}) async-start(f32[8,32,384]{2,1,0:T(8,128)} %bitcast), calls=%async_computation.1 | async-start | bytes 786432 | tf_op jit(solution)/shard_map/all_to_all | solution.py:144
  65.4 12.6 %collective-permute-start.5 = (f32[128,1024]{1,0:T(8,128)S(1)}, f32[128,1024]{1,0:T(8,128)S(1)}, u32[]{:S(2)}, u32[]{:S(2)}) collective-permute-start(f32[128,1024]{1,0:T(8,128)S(1)} %pad_maximum_fusion.refs_0_), channel_id=1, source_target_pairs={{0,32},{32,0},{1,33},{33,1},{2,34},{34,2},{3,35},{35,3},{4,36},{36... | collective-permute-start | bytes 1572872 | tf_op jit(solution)/shard_map/ppermute | solution.py:120
  67.4 10.6 %collective-permute-start.6 = (f32[128,1024]{1,0:T(8,128)S(1)}, f32[128,1024]{1,0:T(8,128)}, u32[]{:S(2)}, u32[]{:S(2)}) collective-permute-start(f32[128,1024]{1,0:T(8,128)S(1)} %collective-permute-done.3.refs_1_), channel_id=1, source_target_pairs={{0,32},{32,0},{1,33},{33,1},{2,34},{34,2},{3,35},{35,3},{4,36},{36... | collective-permute-start | bytes 1572872 | tf_op jit(solution)/shard_map/ppermute | solution.py:120
  69.8 8.2 %collective-permute-start.7 = (f32[128,1024]{1,0:T(8,128)S(1)}, f32[128,1024]{1,0:T(8,128)}, u32[]{:S(2)}, u32[]{:S(2)}) collective-permute-start(f32[128,1024]{1,0:T(8,128)S(1)} %collective-permute-done.4.refs_2_), channel_id=1, source_target_pairs={{0,32},{32,0},{1,33},{33,1},{2,34},{34,2},{3,35},{35,3},{4,36},{36... | collective-permute-start | bytes 1572872 | tf_op jit(solution)/shard_map/ppermute | solution.py:120

commit v2 on v1

v2 whole, which is shorter than its diff:
```python
import functools

import jax
import jax.numpy as jnp
from jax import lax
from jax.experimental import pallas as pl
from jax.experimental.pallas import tpu as pltpu
from jax.sharding import Mesh
from jax.sharding import PartitionSpec as P

BLK = 128
NZ, NCORE, NY, NX = 12, 2, 8, 4
NP, MU, NLOC, L = 24, 16, 4096, 1024
SIG = 32
ROWS = NP * MU
KB = 512
AHEAD = 4
F32, BF16 = jnp.float32, jnp.bfloat16


def coeff_kernel(ahead, mask_ref, three_hbm, dens_hbm, *refs):
    out_hbm, three, dens, acc, out, three_sem, dens_sem, out_sem = refs[-8:]
    z = lax.axis_index("z")

    @pl.when((z < AHEAD) if ahead else (z >= AHEAD))
    def _():
        copies = []
        for i in range(NLOC // KB):
            part = pl.ds(i * KB, KB)
            pair = (
                pltpu.make_async_copy(three_hbm.at[:, :, part], three.at[:, :, part], three_sem.at[i]),
                pltpu.make_async_copy(dens_hbm.at[part], dens.at[part], dens_sem.at[i]),
            )
            for copy in pair:
                copy.start()
            copies.append(pair)
        mask = mask_ref[...].astype(F32)
        for i, pair in enumerate(copies):
            blocks = range(i * KB // BLK, (i + 1) * KB // BLK)
            wide = [jnp.broadcast_to(mask[:, b : b + 1], (MU, BLK)) for b in blocks]
            wide = jnp.concatenate(wide, axis=1).astype(BF16)
            for copy in pair:
                copy.wait()
            masked = (three[:, :, i * KB : (i + 1) * KB] * wide[None]).reshape(ROWS, KB)
            term = jnp.dot(masked, dens[i * KB : (i + 1) * KB, :], preferred_element_type=F32)
            if i == 0:
                acc[...] = term
            elif i < len(copies) - 1:
                acc[...] += term
            else:
                total = acc[...] + term
        backs = []
        for y in range(NY):
            rows = pl.ds(y * SIG, SIG)
            turned = total[:, y * BLK : (y + 1) * BLK].T
            out[:, y * SIG : (y + 1) * SIG, :] = turned.reshape(NX, SIG, ROWS)
            back = pltpu.make_async_copy(out.at[:, rows], out_hbm.at[:, rows], out_sem.at[y])
            back.start()
            backs.append(back)
        for back in backs:
            back.wait()


def partial_coeffs(ahead, pair_mask, three_center, density, *held):
    chunks = NLOC // KB
    anywhere = pl.BlockSpec(memory_space=pl.ANY)
    part = jax.ShapeDtypeStruct((NX, NY * SIG, ROWS), F32)
    return pl.pallas_call(
        functools.partial(coeff_kernel, ahead),
        in_specs=[pl.BlockSpec(memory_space=pltpu.VMEM)] + [anywhere] * (2 + len(held)),
        out_specs=anywhere,
        out_shape=part,
        scratch_shapes=[
            pltpu.VMEM((NP, MU, NLOC), BF16),
            pltpu.VMEM((NLOC, L), BF16),
            pltpu.VMEM((ROWS, L), F32),
            pltpu.VMEM((NX, NY * SIG, ROWS), F32),
            pltpu.SemaphoreType.DMA((chunks,)),
            pltpu.SemaphoreType.DMA((chunks,)),
            pltpu.SemaphoreType.DMA((NY,)),
        ],
        input_output_aliases={} if ahead else {3: 0},
        compiler_params=pltpu.CompilerParams(vmem_limit_bytes=56 * 1024 * 1024),
        cost_estimate=pl.CostEstimate(
            flops=2 * ROWS * NLOC * L, bytes_accessed=13_000_000, transcendentals=0
        ),
    )(pair_mask, three_center, density, *held)


def sum_kernel(got_ref, out_ref):
    for y in range(NY):
        got = got_ref[:, y * SIG : (y + 1) * SIG]
        out_ref[y] = (got[0] + got[1]) + (got[2] + got[3])


def summed(got):
    return pl.pallas_call(
        sum_kernel,
        in_specs=[pl.BlockSpec(memory_space=pltpu.VMEM)],
        out_specs=pl.BlockSpec(memory_space=pltpu.VMEM),
        out_shape=jax.ShapeDtypeStruct((NY, SIG, ROWS), F32),
        compiler_params=pltpu.CompilerParams(vmem_limit_bytes=4 * 1024 * 1024),
        cost_estimate=pl.CostEstimate(
            flops=NX * NY * SIG * ROWS, bytes_accessed=2_000_000, transcendentals=0
        ),
    )(got)


def mixing(z, core, metric):
    slot = lax.broadcasted_iota(jnp.int32, (1, ROWS), 1) // MU
    holder = jnp.where(slot < NZ, core, 1 - core)
    group, kind = (slot % NZ) // 3, slot % 3
    near = jnp.where(group == 0, 0, jnp.where(group == 1, 1, jnp.where(group == 2, 11, 2)))
    away = jnp.where(kind == 0, 0, jnp.where(holder == 0, 4, 8))
    origin = (z + NZ - near + away) % NZ
    slots = origin * NCORE + jnp.where(kind == 2, 1 - holder, holder)
    row = lax.broadcasted_iota(jnp.int32, (ROWS, NP), 0)
    col = lax.broadcasted_iota(jnp.int32, (ROWS, NP), 1)
    expand = ((row // MU) == col).astype(F32).astype(BF16)
    pick = lax.broadcasted_iota(jnp.int32, (NP, ROWS), 0) == slots
    pick = pick.astype(F32).astype(BF16)
    row = lax.broadcasted_iota(jnp.int32, (ROWS, ROWS), 0)
    col = lax.broadcasted_iota(jnp.int32, (ROWS, ROWS), 1)
    same = (row % MU) == (col % MU)
    dot = functools.partial(jnp.dot, preferred_element_type=F32)
    wide = [dot(dot(expand, piece).astype(BF16), pick) for piece in halves(metric.T)]
    return [jnp.where(same, piece, 0.0).astype(BF16) for piece in wide]


def stack_kernel(own_ref, got_ref, far_ref):
    far_ref[:SIG] = own_ref[...]
    far_ref[SIG:] = got_ref[...]


def stacked(own, got):
    local = pl.BlockSpec(memory_space=pltpu.VMEM)
    return pl.pallas_call(
        stack_kernel,
        in_specs=[local] * 2,
        out_specs=local,
        out_shape=jax.ShapeDtypeStruct((3 * SIG, L), F32),
        compiler_params=pltpu.CompilerParams(vmem_limit_bytes=8 * 1024 * 1024),
        cost_estimate=pl.CostEstimate(
            flops=40_000_000_000, bytes_accessed=2_000_000, transcendentals=0
        ),
    )(own, got)


def halves(a):
    top = a.astype(BF16)
    return top, (a - top.astype(F32)).astype(BF16)


def dot3(a, b):
    a_top, a_low = halves(a)
    b_top, b_low = halves(b)
    dot = functools.partial(jnp.dot, preferred_element_type=F32)
    return dot(a_top, b_top) + (dot(a_low, b_top) + dot(a_top, b_low))


def exchange_kernel(parts_ref, metric_ref, *refs):
    aux_refs, out_ref = refs[:-1], refs[-1]
    mix_top, mix_low = mixing(lax.axis_index("z"), lax.axis_index("core"), metric_ref[...])
    dot = functools.partial(jnp.dot, preferred_element_type=F32)
    coeffs = parts_ref[0]
    for y in range(1, NY):
        coeffs = coeffs + parts_ref[y]
    top, low = halves(coeffs)
    fitted = dot(top, mix_top) + (dot(low, mix_top) + dot(top, mix_low))
    fitted = fitted.T
    total = None
    for g, aux_ref in enumerate(aux_refs):
        slots = range(g * 3, (g + 1) * 3)
        left = jnp.concatenate([fitted[s * MU : (s + 1) * MU] for s in slots], axis=1)
        term = dot3(left, aux_ref[...])
        total = term if total is None else total + term
    for c in range(NY * NX):
        lane, row = (c // 4) * BLK, (c % 4) * 4
        out_ref[c] = total[row : row + 4, lane : lane + BLK]


def exchange_partial(parts, metric, aux_groups):
    local = pl.BlockSpec(memory_space=pltpu.VMEM)
    return pl.pallas_call(
        exchange_kernel,
        in_specs=[local] * (2 + len(aux_groups)),
        out_specs=local,
        out_shape=jax.ShapeDtypeStruct((NY * NX, 4, BLK), F32),
        compiler_params=pltpu.CompilerParams(vmem_limit_bytes=16 * 1024 * 1024),
        cost_estimate=pl.CostEstimate(
            flops=6 * MU * NP * SIG * L, bytes_accessed=4_000_000, transcendentals=0
        ),
    )(parts, metric, *aux_groups)


def shift(a, axis, size, by):
    return lax.ppermute(a, axis, [(i, (i + by) % size) for i in range(size)])


def on_device(three_center, density, pair_mask, metric, aux_pairs):
    own = aux_pairs.reshape(SIG, L)
    part = partial_coeffs(True, pair_mask, three_center, density)
    own, part = lax.optimization_barrier((own, part))
    both = jnp.concatenate([own, shift(own, "core", NCORE, 1)], axis=0)
    ways = [
        (z * NCORE + core, (z + (8, 4)[core]) % NZ * NCORE + core)
        for z in range(NZ)
        for core in range(NCORE)
    ]
    far = stacked(own, lax.ppermute(both, ("z", "core"), ways))
    groups = [far, *[shift(far, "z", NZ, by) for by in (1, 11, 2)]]
    groups += [shift(g, "core", NCORE, 1) for g in groups]
    part = partial_coeffs(False, pair_mask, three_center, density, part)

    got = lax.all_to_all(part, "x", 0, 0, tiled=True)
    near = summed(got)
    got = lax.all_to_all(near, "y", 0, 0, tiled=True)
    term = exchange_partial(got, metric, groups)
    got = lax.all_to_all(term, ("y", "x"), 0, 0, tiled=True)
    done = jnp.broadcast_to(jnp.sum(got, axis=0)[None], (NY * NX, 4, BLK))
    full = lax.all_to_all(done, ("y", "x"), 0, 0, tiled=True)
    return full.reshape(8, MU, BLK).transpose(1, 0, 2).reshape(MU, L)


def solution(mesh):
    grid = Mesh(mesh.devices.reshape(NZ, NCORE, NY, NX), ("z", "core", "y", "x"))
    row, col = ("z", "core"), ("y", "x")
    placed = (P(None, row, col), P(col, None), P(row, col), P(), P(row, col, None))
    return jax.shard_map(
        on_device, mesh=grid, in_specs=placed, out_specs=P(row, None), check_vma=False
    )
```

time: 114 us -> 100 us (0.88)
  starting transfers between devices: 47.9 us -> 42.5 us
  local copies, waits for them, and re-layouts: 4.88 us -> 0.66 us
  other arithmetic: 3.73 us -> 0.06 us
  Pallas kernels: 13.7 us -> 11.1 us
  waiting for transfers between devices: 10.9 us -> 13.2 us
    ppermute x8, starting transfers between devices: 36.1 us -> 21.2 us  [shift(): return lax.ppermute(a, axis, [(i, (i + by) % size) for i in range(size)])]
    ppermute x0 -> x1, starting transfers between devices: none -> 8.31 us  [on_device(): far = stacked(own, lax.ppermute(both, ('z', 'core'), ways))]
    ppermute x0 -> x1, waiting for transfers between devices: none -> 7.19 us  [on_device(): far = stacked(own, lax.ppermute(both, ('z', 'core'), ways))]
    ppermute x8, waiting for transfers between devices: 10.9 us -> 5.68 us  [shift(): return lax.ppermute(a, axis, [(i, (i + by) % size) for i in range(size)])]
    mul x1 -> x0, local copies, waits for them, and re-layouts: 3.58 us -> none  [on_device(): mix = chosen.T[:, None, :, None] * jnp.eye(MU, dtype=F32)[None, :, None, :]]
    pallas_call x2 -> x5, Pallas kernels: 13.7 us -> 11.1 us  [the longest x2 8.11 us: partial_coeffs(): pl.pallas_call(functools.partial(coeff_kernel, ahead), in_specs=[pl.Block...]
    mul x1 -> x0, other arithmetic: 2.52 us -> none  [on_device(): mix = chosen.T[:, None, :, None] * jnp.eye(MU, dtype=F32)[None, :, None, :]]
  transfers between devices with their start and end apart: 10 -> 11, of which waited for: 1 -> 6; matrix products, arithmetic and copies ran while one was open for 7% -> 0% of each run, Pallas kernels for 0% -> 2%
where the time goes in v2:
time: 100 us; the launch traced here: 99.4 us
  starting transfers between devices  42.5 us (42%)
  blocking collectives  31.7 us (32%)
  waiting for transfers between devices  13.2 us (13%)
  Pallas kernels  11.1 us (11%)
    ppermute x8, starting transfers between devices, shift(): return lax.ppermute(a, axis, [(i, (i + by) % size) for i in range(size)])  21.2 us
    all_to_all x1, blocking collectives, on_device(): got = lax.all_to_all(term, ('y', 'x'), 0, 0, tiled=True)  18.7 us
    all_to_all x1, blocking collectives, on_device(): full = lax.all_to_all(done, ('y', 'x'), 0, 0, tiled=True)  13.1 us
    all_to_all x1, starting transfers between devices, on_device(): got = lax.all_to_all(near, 'y', 0, 0, tiled=True)  8.65 us
    ppermute x1, starting transfers between devices, on_device(): far = stacked(own, lax.ppermute(both, ('z', 'core'), ways))  8.31 us
    pallas_call x2, Pallas kernels, partial_coeffs(): pl.pallas_call(functools.partial(coeff_kernel, ahead), in_specs=[pl.Block...  8.11 us
    ppermute x1, waiting for transfers between devices, on_device(): far = stacked(own, lax.ppermute(both, ('z', 'core'), ways))  7.19 us
    ppermute x8, waiting for transfers between devices, shift(): return lax.ppermute(a, axis, [(i, (i + by) % size) for i in range(size)])  5.68 us
  transfers between devices with their start and end apart: 11, of which 6 were waited for; matrix products, arithmetic and copies ran while one was open for 0% of the time, Pallas kernels for 2%

profile of v2, /device:TPU:8, one launch (start us, length us, event | category | flops | bytes accessed | tf_op | source)
XLA Modules:
  0.0 99.4 jit_solution(3807632429191146333)
XLA Ops:
  0.0 7.2 %shard_map.55.refs_0_ = f32[4,256,384]{2,1,0:T(8,128)} custom-call(s32[16,32]{1,0:T(8,128)} %mask_ref.3, bf16[24,16,4096]{2,1,0:T(8,128)(2,1)} %three_hbm.3, bf16[4096,1024]{1,0:T(8,128)(2,1)} %dens_hbm.3), custom_call_target="tpu_custom_call" | custom-call | flops 3221225472 | bytes 13000000 | tf_op jit(solution)/shard_map/pallas_call | solution.py:68
  7.2 0.0 copy-done
  7.2 1.9 %collective-permute-start = (f32[32,1024]{1,0:T(8,128)S(1)}, f32[32,1024]{1,0:T(8,128)S(1)}, u32[]{:S(2)}, u32[]{:S(2)}) collective-permute-start(f32[32,1024]{1,0:T(8,128)S(1)} %bitcast.8), channel_id=1, source_target_pairs={{0,32},{32,0},{1,33},{33,1},{2,34},{34,2},{3,35},{35,3},{4,36},{36... | collective-permute-start | bytes 393224 | tf_op jit(solution)/shard_map/ppermute | solution.py:197
  9.1 1.3 %collective-permute-done = f32[32,1024]{1,0:T(8,128)S(1)} collective-permute-done((f32[32,1024]{1,0:T(8,128)S(1)}, f32[32,1024]{1,0:T(8,128)S(1)}, u32[]{:S(2)}, u32[]{:S(2)}) %collective-permute-start) | collective-permute-done | bytes 131104 | tf_op jit(solution)/shard_map/ppermute | solution.py:197
  10.5 8.3 %collective-permute-start.1 = (f32[64,1024]{1,0:T(8,128)S(1)}, f32[64,1024]{1,0:T(8,128)S(1)}, u32[]{:S(2)}, u32[]{:S(2)}) collective-permute-start(f32[64,1024]{1,0:T(8,128)S(1)} %pad_maximum_fusion), channel_id=1, source_target_pairs={{0,512},{32,288},{64,576},{96,352},{128,640},{160,416},{192,704},{... | collective-permute-start | bytes 786440 | tf_op jit(solution)/shard_map/ppermute | solution.py:210
  18.8 0.9 shard_map.56
  19.7 4.3 %all-to-all-start = ((f32[4,256,384]{2,1,0:T(8,128)}), f32[4,256,384]{2,1,0:T(8,128)S(1)}, u32[]{:S(2)}, u32[]{:S(2)}) async-start(f32[4,256,384]{2,1,0:T(8,128)} %shard_map.56), calls=%async_computation | async-start | bytes 3145728 | tf_op jit(solution)/shard_map/all_to_all | solution.py:215
  24.0 7.2 %collective-permute-done.1.got_ref = f32[64,1024]{1,0:T(8,128)S(1)} collective-permute-done((f32[64,1024]{1,0:T(8,128)S(1)}, f32[64,1024]{1,0:T(8,128)S(1)}, u32[]{:S(2)}, u32[]{:S(2)}) %collective-permute-start.1) | collective-permute-done | bytes 262176 | tf_op jit(solution)/shard_map/ppermute | solution.py:210
  31.2 0.0 copy-start.1
  31.3 5.2 %collective-permute-start.4 = (f32[96,1024]{1,0:T(8,128)S(1)}, f32[96,1024]{1,0:T(8,128)S(1)}, u32[]{:S(2)}, u32[]{:S(2)}) collective-permute-start(f32[96,1024]{1,0:T(8,128)S(1)} %shard_map.58.refs_0_), channel_id=1, source_target_pairs={{0,128},{64,192},{128,256},{192,320},{256,384},{320,448},{384,512}... | collective-permute-start | bytes 1179656 | tf_op jit(solution)/shard_map/ppermute | solution.py:197
  36.5 1.9 %collective-permute-start.3 = (f32[96,1024]{1,0:T(8,128)S(1)}, f32[96,1024]{1,0:T(8,128)S(1)}, u32[]{:S(2)}, u32[]{:S(2)}) collective-permute-start(f32[96,1024]{1,0:T(8,128)S(1)} %shard_map.58.refs_0_), channel_id=1, source_target_pairs={{0,704},{64,0},{128,64},{192,128},{256,192},{320,256},{384,320},{4... | collective-permute-start | bytes 1179656 | tf_op jit(solution)/shard_map/ppermute | solution.py:197
  38.4 3.9 %collective-permute-start.2 = (f32[96,1024]{1,0:T(8,128)S(1)}, f32[96,1024]{1,0:T(8,128)S(1)}, u32[]{:S(2)}, u32[]{:S(2)}) collective-permute-start(f32[96,1024]{1,0:T(8,128)S(1)} %shard_map.58.refs_0_), channel_id=1, source_target_pairs={{0,64},{64,128},{128,192},{192,256},{256,320},{320,384},{384,448},... | collective-permute-start | bytes 1179656 | tf_op jit(solution)/shard_map/ppermute | solution.py:197
  42.3 0.0 all-to-all-done.got_ref
  42.4 0.8 shard_map.57
  43.2 8.6 %all-to-all-start.1 = ((f32[8,32,384]{2,1,0:T(8,128)}), f32[8,32,384]{2,1,0:T(8,128)S(1)}, u32[]{:S(2)}, u32[]{:S(2)}) async-start(f32[8,32,384]{2,1,0:T(8,128)} %shard_map.57), calls=%async_computation.1 | async-start | bytes 786432 | tf_op jit(solution)/shard_map/all_to_all | solution.py:217
  51.8 1.9 %collective-permute-start.5 = (f32[96,1024]{1,0:T(8,128)S(1)}, f32[96,1024]{1,0:T(8,128)S(1)}, u32[]{:S(2)}, u32[]{:S(2)}) collective-permute-start(f32[96,1024]{1,0:T(8,128)S(1)} %shard_map.58.refs_0_), channel_id=1, source_target_pairs={{0,32},{32,0},{1,33},{33,1},{2,34},{34,2},{3,35},{35,3},{4,36},{36... | collective-permute-start | bytes 1179656 | tf_op jit(solution)/shard_map/ppermute | solution.py:197
  53.7 1.0 collective-permute-done.4.refs_3_
  54.7 1.9 %collective-permute-start.8 = (f32[96,1024]{1,0:T(8,128)S(1)}, f32[96,1024]{1,0:T(8,128)S(1)}, u32[]{:S(2)}, u32[]{:S(2)}) collective-permute-start(f32[96,1024]{1,0:T(8,128)S(1)} %collective-permute-done.4.refs_3_), channel_id=1, source_target_pairs={{0,32},{32,0},{1,33},{33,1},{2,34},{34,2},{3,35},{35,3},{4,36},{36... | collective-permute-start | bytes 1179656 | tf_op jit(solution)/shard_map/ppermute | solution.py:197
  56.6 0.0 collective-permute-done.3.refs_2_
  56.6 2.4 %collective-permute-start.7 = (f32[96,1024]{1,0:T(8,128)S(1)}, f32[96,1024]{1,0:T(8,128)S(1)}, u32[]{:S(2)}, u32[]{:S(2)}) collective-permute-start(f32[96,1024]{1,0:T(8,128)S(1)} %collective-permute-done.3.refs_2_), channel_id=1, source_target_pairs={{0,32},{32,0},{1,33},{33,1},{2,34},{34,2},{3,35},{35,3},{4,36},{36... | collective-permute-start | bytes 1179656 | tf_op jit(solution)/shard_map/ppermute | solution.py:197
  59.0 1.9 %collective-permute-done.2.refs_1_ = f32[96,1024]{1,0:T(8,128)S(1)} collective-permute-done((f32[96,1024]{1,0:T(8,128)S(1)}, f32[96,1024]{1,0:T(8,128)S(1)}, u32[]{:S(2)}, u32[]{:S(2)}) %collective-permute-start.2) | collective-permute-done | bytes 393248 | tf_op jit(solution)/shard_map/ppermute | solution.py:197
  60.9 2.0 %collective-permute-start.6 = (f32[96,1024]{1,0:T(8,128)S(1)}, f32[96,1024]{1,0:T(8,128)S(1)}, u32[]{:S(2)}, u32[]{:S(2)}) collective-permute-start(f32[96,1024]{1,0:T(8,128)S(1)} %collective-permute-done.2.refs_1_), channel_id=1, source_target_pairs={{0,32},{32,0},{1,33},{33,1},{2,34},{34,2},{3,35},{35,3},{4,36},{36... | collective-permute-start | bytes 1179656 | tf_op jit(solution)/shard_map/ppermute | solution.py:197
  62.9 0.0 collective-permute-done.5.refs_4_
  62.9 0.0 collective-permute-done.8.refs_7_
  62.9 0.0 collective-permute-done.7.refs_6_
  62.9 1.6 %collective-permute-done.6.refs_5_ = f32[96,1024]{1,0:T(8,128)S(1)} collective-permute-done((f32[96,1024]{1,0:T(8,128)S(1)}, f32[96,1024]{1,0:T(8,128)S(1)}, u32[]{:S(2)}, u32[]{:S(2)}) %collective-permute-start.6) | collective-permute-done | bytes 393248 | tf_op jit(solution)/shard_map/ppermute | solution.py:197
  64.5 0.3 all-to-all-done.1.parts_ref
  64.8 0.0 copy-done.1
  64.8 2.2 %shard_map.59 = f32[32,4,128]{2,1,0:T(4,128)S(1)} custom-call(f32[8,32,384]{2,1,0:T(8,128)S(1)} %all-to-all-done.1.parts_ref, f32[24,24]{1,0:T(8,128)S(1)} %copy-done.1, f32[96,1024]{1,0:T(8,128)S(1)} %shard_map.58.refs_0_, f32[96,1024]{1,0:T(8,128)S(1)} %collective-permute-done.2.refs_1_, f32[96,1024]{1,0:T(8,128)S(1)} %collective-permute-done.3.refs_2_, ...), custom_call_target="tpu_custom_call" | custom-call | flops 75497472 | bytes 4000000 | tf_op jit(solution)/shard_map/pallas_call | solution.py:184
  67.0 18.7 %all_to_all.20 = f32[32,4,128]{2,1,0:T(4,128)S(1)} all-to-all(f32[32,4,128]{2,1,0:T(4,128)S(1)} %shard_map.59), channel_id=1, replica_groups=mesh['z'=12,'core'=2,'y'=8,'x'=4] {'y','x'}, dimensions={0} | all-to-all | bytes 131072 | tf_op jit(solution)/shard_map/all_to_all | solution.py:219
  85.7 13.1 %all_to_all.21 = f32[32,4,128]{2,1,0:T(4,128)S(1)} all-to-all(f32[32,4,128]{2,1,0:T(4,128)S(1)} %broadcast_in_dim.2), channel_id=1, replica_groups=mesh['z'=12,'core'=2,'y'=8,'x'=4] {'y','x'}, dimensions={0} | all-to-all | bytes 131072 | tf_op jit(solution)/shard_map/all_to_all | solution.py:221
  98.8 0.6 copy.10
  (5 shorter events, 0.1 us)
Async XLA Ops:
  0.0 7.2 %copy-start = (f32[1,32,1024]{2,1,0:T(8,128)S(1)}, f32[1,32,1024]{2,1,0:T(8,128)}, u32[]{:S(2)}) copy-start(f32[1,32,1024]{2,1,0:T(8,128)} %param.9) | copy-start | bytes 393220
  7.2 3.2 %collective-permute-start = (f32[32,1024]{1,0:T(8,128)S(1)}, f32[32,1024]{1,0:T(8,128)S(1)}, u32[]{:S(2)}, u32[]{:S(2)}) collective-permute-start(f32[32,1024]{1,0:T(8,128)S(1)} %bitcast.8), channel_id=1, source_target_pairs={{0,32},{32,0},{1,33},{33,1},{2,34},{34,2},{3,35},{35,3},{4,36},{36... | collective-permute-start | bytes 393224 | tf_op jit(solution)/shard_map/ppermute | solution.py:197
  10.5 20.7 %collective-permute-start.1 = (f32[64,1024]{1,0:T(8,128)S(1)}, f32[64,1024]{1,0:T(8,128)S(1)}, u32[]{:S(2)}, u32[]{:S(2)}) collective-permute-start(f32[64,1024]{1,0:T(8,128)S(1)} %pad_maximum_fusion), channel_id=1, source_target_pairs={{0,512},{32,288},{64,576},{96,352},{128,640},{160,416},{192,704},{... | collective-permute-start | bytes 786440 | tf_op jit(solution)/shard_map/ppermute | solution.py:210
  19.7 22.6 %all-to-all-start = ((f32[4,256,384]{2,1,0:T(8,128)}), f32[4,256,384]{2,1,0:T(8,128)S(1)}, u32[]{:S(2)}, u32[]{:S(2)}) async-start(f32[4,256,384]{2,1,0:T(8,128)} %shard_map.56), calls=%async_computation | async-start | bytes 3145728 | tf_op jit(solution)/shard_map/all_to_all | solution.py:215
  31.2 33.6 %copy-start.1 = (f32[24,24]{1,0:T(8,128)S(1)}, f32[24,24]{1,0:T(8,128)}, u32[]{:S(2)}) copy-start(f32[24,24]{1,0:T(8,128)} %metric_ref.1) | copy-start | bytes 6916
  31.3 23.4 %collective-permute-start.4 = (f32[96,1024]{1,0:T(8,128)S(1)}, f32[96,1024]{1,0:T(8,128)S(1)}, u32[]{:S(2)}, u32[]{:S(2)}) collective-permute-start(f32[96,1024]{1,0:T(8,128)S(1)} %shard_map.58.refs_0_), channel_id=1, source_target_pairs={{0,128},{64,192},{128,256},{192,320},{256,384},{320,448},{384,512}... | collective-permute-start | bytes 1179656 | tf_op jit(solution)/shard_map/ppermute | solution.py:197
  36.5 20.1 %collective-permute-start.3 = (f32[96,1024]{1,0:T(8,128)S(1)}, f32[96,1024]{1,0:T(8,128)S(1)}, u32[]{:S(2)}, u32[]{:S(2)}) collective-permute-start(f32[96,1024]{1,0:T(8,128)S(1)} %shard_map.58.refs_0_), channel_id=1, source_target_pairs={{0,704},{64,0},{128,64},{192,128},{256,192},{320,256},{384,320},{4... | collective-permute-start | bytes 1179656 | tf_op jit(solution)/shard_map/ppermute | solution.py:197
  38.4 22.5 %collective-permute-start.2 = (f32[96,1024]{1,0:T(8,128)S(1)}, f32[96,1024]{1,0:T(8,128)S(1)}, u32[]{:S(2)}, u32[]{:S(2)}) collective-permute-start(f32[96,1024]{1,0:T(8,128)S(1)} %shard_map.58.refs_0_), channel_id=1, source_target_pairs={{0,64},{64,128},{128,192},{192,256},{256,320},{320,384},{384,448},... | collective-permute-start | bytes 1179656 | tf_op jit(solution)/shard_map/ppermute | solution.py:197
  43.2 21.7 %all-to-all-start.1 = ((f32[8,32,384]{2,1,0:T(8,128)}), f32[8,32,384]{2,1,0:T(8,128)S(1)}, u32[]{:S(2)}, u32[]{:S(2)}) async-start(f32[8,32,384]{2,1,0:T(8,128)} %shard_map.57), calls=%async_computation.1 | async-start | bytes 786432 | tf_op jit(solution)/shard_map/all_to_all | solution.py:217
  51.8 11.1 %collective-permute-start.5 = (f32[96,1024]{1,0:T(8,128)S(1)}, f32[96,1024]{1,0:T(8,128)S(1)}, u32[]{:S(2)}, u32[]{:S(2)}) collective-permute-start(f32[96,1024]{1,0:T(8,128)S(1)} %shard_map.58.refs_0_), channel_id=1, source_target_pairs={{0,32},{32,0},{1,33},{33,1},{2,34},{34,2},{3,35},{35,3},{4,36},{36... | collective-permute-start | bytes 1179656 | tf_op jit(solution)/shard_map/ppermute | solution.py:197
  54.7 8.2 %collective-permute-start.8 = (f32[96,1024]{1,0:T(8,128)S(1)}, f32[96,1024]{1,0:T(8,128)S(1)}, u32[]{:S(2)}, u32[]{:S(2)}) collective-permute-start(f32[96,1024]{1,0:T(8,128)S(1)} %collective-permute-done.4.refs_3_), channel_id=1, source_target_pairs={{0,32},{32,0},{1,33},{33,1},{2,34},{34,2},{3,35},{35,3},{4,36},{36... | collective-permute-start | bytes 1179656 | tf_op jit(solution)/shard_map/ppermute | solution.py:197
  56.6 6.3 %collective-permute-start.7 = (f32[96,1024]{1,0:T(8,128)S(1)}, f32[96,1024]{1,0:T(8,128)S(1)}, u32[]{:S(2)}, u32[]{:S(2)}) collective-permute-start(f32[96,1024]{1,0:T(8,128)S(1)} %collective-permute-done.3.refs_2_), channel_id=1, source_target_pairs={{0,32},{32,0},{1,33},{33,1},{2,34},{34,2},{3,35},{35,3},{4,36},{36... | collective-permute-start | bytes 1179656 | tf_op jit(solution)/shard_map/ppermute | solution.py:197
  60.9 3.6 %collective-permute-start.6 = (f32[96,1024]{1,0:T(8,128)S(1)}, f32[96,1024]{1,0:T(8,128)S(1)}, u32[]{:S(2)}, u32[]{:S(2)}) collective-permute-start(f32[96,1024]{1,0:T(8,128)S(1)} %collective-permute-done.2.refs_1_), channel_id=1, source_target_pairs={{0,32},{32,0},{1,33},{33,1},{2,34},{34,2},{3,35},{35,3},{4,36},{36... | collective-permute-start | bytes 1179656 | tf_op jit(solution)/shard_map/ppermute | solution.py:197

commit v3 on v2

--- a/solution.py
+++ b/solution.py
@@ -175,7 +175,7 @@
         term = dot3(left, aux_ref[...])
         total = term if total is None else total + term
     for c in range(NY * NX):
-        lane, row = (c // 4) * BLK, (c % 4) * 4
+        lane, row = (c % 16) // 2 * BLK, (c // 16) * 8 + (c % 2) * 4
         out_ref[c] = total[row : row + 4, lane : lane + BLK]
 
 
@@ -199,9 +199,10 @@
 
 def on_device(three_center, density, pair_mask, metric, aux_pairs):
     own = aux_pairs.reshape(SIG, L)
+    swap = shift(own, "core", NCORE, 1)
     part = partial_coeffs(True, pair_mask, three_center, density)
-    own, part = lax.optimization_barrier((own, part))
-    both = jnp.concatenate([own, shift(own, "core", NCORE, 1)], axis=0)
+    own, swap, part = lax.optimization_barrier((own, swap, part))
+    both = jnp.concatenate([own, swap], axis=0)
     ways = [
         (z * NCORE + core, (z + (8, 4)[core]) % NZ * NCORE + core)
         for z in range(NZ)
@@ -219,7 +220,7 @@
     got = lax.all_to_all(term, ("y", "x"), 0, 0, tiled=True)
     done = jnp.broadcast_to(jnp.sum(got, axis=0)[None], (NY * NX, 4, BLK))
     full = lax.all_to_all(done, ("y", "x"), 0, 0, tiled=True)
-    return full.reshape(8, MU, BLK).transpose(1, 0, 2).reshape(MU, L)
+    return full.reshape(2, 8, 8, BLK).transpose(0, 2, 1, 3).reshape(MU, L)
 
 
 def solution(mesh):

time: 100 us -> 99.5 us (level)
    ppermute x8, waiting for transfers between devices: 5.68 us -> 4.65 us  [shift(): return lax.ppermute(a, axis, [(i, (i + by) % size) for i in range(size)])]
  transfers between devices with their start and end apart: 11 -> 11, of which waited for: 6 -> 5; matrix products, arithmetic and copies ran while one was open for 0% -> 0% of each run, Pallas kernels for 2% -> 9%
where the time goes in v3:
time: 99.5 us; the launch traced here: 98.8 us
  starting transfers between devices  42.9 us (43%)
  blocking collectives  31.6 us (32%)
  waiting for transfers between devices  12.3 us (12%)
  Pallas kernels  11.1 us (11%)
    ppermute x8, starting transfers between devices, shift(): return lax.ppermute(a, axis, [(i, (i + by) % size) for i in range(size)])  21.3 us
    all_to_all x1, blocking collectives, on_device(): got = lax.all_to_all(term, ('y', 'x'), 0, 0, tiled=True)  18.6 us
    all_to_all x1, blocking collectives, on_device(): full = lax.all_to_all(done, ('y', 'x'), 0, 0, tiled=True)  13.1 us
    ppermute x1, starting transfers between devices, on_device(): far = stacked(own, lax.ppermute(both, ('z', 'core'), ways))  8.89 us
    all_to_all x1, starting transfers between devices, on_device(): got = lax.all_to_all(near, 'y', 0, 0, tiled=True)  8.42 us
    pallas_call x2, Pallas kernels, partial_coeffs(): pl.pallas_call(functools.partial(coeff_kernel, ahead), in_specs=[pl.Block...  8.08 us
    ppermute x1, waiting for transfers between devices, on_device(): far = stacked(own, lax.ppermute(both, ('z', 'core'), ways))  7.19 us
    ppermute x8, waiting for transfers between devices, shift(): return lax.ppermute(a, axis, [(i, (i + by) % size) for i in range(size)])  4.65 us
  transfers between devices with their start and end apart: 11, of which 5 were waited for; matrix products, arithmetic and copies ran while one was open for 0% of the time, Pallas kernels for 9%

profile of v3, /device:TPU:8, one launch (start us, length us, event | category | flops | bytes accessed | tf_op | source)
XLA Modules:
  0.0 98.8 jit_solution(8556747344452678241)
XLA Ops:
  0.0 2.0 %collective-permute-start = (f32[32,1024]{1,0:T(8,128)}, f32[32,1024]{1,0:T(8,128)S(1)}, u32[]{:S(2)}, u32[]{:S(2)}) collective-permute-start(f32[32,1024]{1,0:T(8,128)} %bitcast.6), channel_id=1, source_target_pairs={{0,32},{32,0},{1,33},{33,1},{2,34},{34,2},{3,35},{35,3},{4,36},{36... | collective-permute-start | bytes 393224 | tf_op jit(solution)/shard_map/ppermute | solution.py:197
  2.0 7.2 %shard_map.55.refs_0_ = f32[4,256,384]{2,1,0:T(8,128)} custom-call(s32[16,32]{1,0:T(8,128)} %mask_ref.3, bf16[24,16,4096]{2,1,0:T(8,128)(2,1)} %three_hbm.3, bf16[4096,1024]{1,0:T(8,128)(2,1)} %dens_hbm.3), custom_call_target="tpu_custom_call" | custom-call | flops 3221225472 | bytes 13000000 | tf_op jit(solution)/shard_map/pallas_call | solution.py:68
  9.2 0.0 collective-permute-done
  9.2 0.0 copy-done
  9.3 8.9 %collective-permute-start.1 = (f32[64,1024]{1,0:T(8,128)S(1)}, f32[64,1024]{1,0:T(8,128)S(1)}, u32[]{:S(2)}, u32[]{:S(2)}) collective-permute-start(f32[64,1024]{1,0:T(8,128)S(1)} %pad_maximum_fusion), channel_id=1, source_target_pairs={{0,512},{32,288},{64,576},{96,352},{128,640},{160,416},{192,704},{... | collective-permute-start | bytes 786440 | tf_op jit(solution)/shard_map/ppermute | solution.py:211
  18.2 0.9 shard_map.56
  19.1 4.3 %all-to-all-start = ((f32[4,256,384]{2,1,0:T(8,128)}), f32[4,256,384]{2,1,0:T(8,128)S(1)}, u32[]{:S(2)}, u32[]{:S(2)}) async-start(f32[4,256,384]{2,1,0:T(8,128)} %shard_map.56), calls=%async_computation | async-start | bytes 3145728 | tf_op jit(solution)/shard_map/all_to_all | solution.py:216
  23.4 7.2 %collective-permute-done.1.got_ref = f32[64,1024]{1,0:T(8,128)S(1)} collective-permute-done((f32[64,1024]{1,0:T(8,128)S(1)}, f32[64,1024]{1,0:T(8,128)S(1)}, u32[]{:S(2)}, u32[]{:S(2)}) %collective-permute-start.1) | collective-permute-done | bytes 262176 | tf_op jit(solution)/shard_map/ppermute | solution.py:211
  30.6 0.0 copy-start.1
  30.6 5.2 %collective-permute-start.4 = (f32[96,1024]{1,0:T(8,128)S(1)}, f32[96,1024]{1,0:T(8,128)S(1)}, u32[]{:S(2)}, u32[]{:S(2)}) collective-permute-start(f32[96,1024]{1,0:T(8,128)S(1)} %shard_map.58.refs_0_), channel_id=1, source_target_pairs={{0,128},{64,192},{128,256},{192,320},{256,384},{320,448},{384,512}... | collective-permute-start | bytes 1179656 | tf_op jit(solution)/shard_map/ppermute | solution.py:197
  35.9 1.9 %collective-permute-start.3 = (f32[96,1024]{1,0:T(8,128)S(1)}, f32[96,1024]{1,0:T(8,128)S(1)}, u32[]{:S(2)}, u32[]{:S(2)}) collective-permute-start(f32[96,1024]{1,0:T(8,128)S(1)} %shard_map.58.refs_0_), channel_id=1, source_target_pairs={{0,704},{64,0},{128,64},{192,128},{256,192},{320,256},{384,320},{4... | collective-permute-start | bytes 1179656 | tf_op jit(solution)/shard_map/ppermute | solution.py:197
  37.8 3.9 %collective-permute-start.2 = (f32[96,1024]{1,0:T(8,128)S(1)}, f32[96,1024]{1,0:T(8,128)S(1)}, u32[]{:S(2)}, u32[]{:S(2)}) collective-permute-start(f32[96,1024]{1,0:T(8,128)S(1)} %shard_map.58.refs_0_), channel_id=1, source_target_pairs={{0,64},{64,128},{128,192},{192,256},{256,320},{320,384},{384,448},... | collective-permute-start | bytes 1179656 | tf_op jit(solution)/shard_map/ppermute | solution.py:197
  41.7 0.0 all-to-all-done.got_ref
  41.7 0.8 shard_map.57
  42.5 8.4 %all-to-all-start.1 = ((f32[8,32,384]{2,1,0:T(8,128)}), f32[8,32,384]{2,1,0:T(8,128)S(1)}, u32[]{:S(2)}, u32[]{:S(2)}) async-start(f32[8,32,384]{2,1,0:T(8,128)} %shard_map.57), calls=%async_computation.1 | async-start | bytes 786432 | tf_op jit(solution)/shard_map/all_to_all | solution.py:218
  51.0 1.9 %collective-permute-start.5 = (f32[96,1024]{1,0:T(8,128)S(1)}, f32[96,1024]{1,0:T(8,128)S(1)}, u32[]{:S(2)}, u32[]{:S(2)}) collective-permute-start(f32[96,1024]{1,0:T(8,128)S(1)} %shard_map.58.refs_0_), channel_id=1, source_target_pairs={{0,32},{32,0},{1,33},{33,1},{2,34},{34,2},{3,35},{35,3},{4,36},{36... | collective-permute-start | bytes 1179656 | tf_op jit(solution)/shard_map/ppermute | solution.py:197
  52.9 1.4 %collective-permute-done.4.refs_3_ = f32[96,1024]{1,0:T(8,128)S(1)} collective-permute-done((f32[96,1024]{1,0:T(8,128)S(1)}, f32[96,1024]{1,0:T(8,128)S(1)}, u32[]{:S(2)}, u32[]{:S(2)}) %collective-permute-start.4) | collective-permute-done | bytes 393248 | tf_op jit(solution)/shard_map/ppermute | solution.py:197
  54.2 1.9 %collective-permute-start.8 = (f32[96,1024]{1,0:T(8,128)S(1)}, f32[96,1024]{1,0:T(8,128)S(1)}, u32[]{:S(2)}, u32[]{:S(2)}) collective-permute-start(f32[96,1024]{1,0:T(8,128)S(1)} %collective-permute-done.4.refs_3_), channel_id=1, source_target_pairs={{0,32},{32,0},{1,33},{33,1},{2,34},{34,2},{3,35},{35,3},{4,36},{36... | collective-permute-start | bytes 1179656 | tf_op jit(solution)/shard_map/ppermute | solution.py:197
  56.1 0.0 collective-permute-done.3.refs_2_
  56.2 2.4 %collective-permute-start.7 = (f32[96,1024]{1,0:T(8,128)S(1)}, f32[96,1024]{1,0:T(8,128)S(1)}, u32[]{:S(2)}, u32[]{:S(2)}) collective-permute-start(f32[96,1024]{1,0:T(8,128)S(1)} %collective-permute-done.3.refs_2_), channel_id=1, source_target_pairs={{0,32},{32,0},{1,33},{33,1},{2,34},{34,2},{3,35},{35,3},{4,36},{36... | collective-permute-start | bytes 1179656 | tf_op jit(solution)/shard_map/ppermute | solution.py:197
  58.6 1.7 %collective-permute-done.2.refs_1_ = f32[96,1024]{1,0:T(8,128)S(1)} collective-permute-done((f32[96,1024]{1,0:T(8,128)S(1)}, f32[96,1024]{1,0:T(8,128)S(1)}, u32[]{:S(2)}, u32[]{:S(2)}) %collective-permute-start.2) | collective-permute-done | bytes 393248 | tf_op jit(solution)/shard_map/ppermute | solution.py:197
  60.3 2.0 %collective-permute-start.6 = (f32[96,1024]{1,0:T(8,128)S(1)}, f32[96,1024]{1,0:T(8,128)S(1)}, u32[]{:S(2)}, u32[]{:S(2)}) collective-permute-start(f32[96,1024]{1,0:T(8,128)S(1)} %collective-permute-done.2.refs_1_), channel_id=1, source_target_pairs={{0,32},{32,0},{1,33},{33,1},{2,34},{34,2},{3,35},{35,3},{4,36},{36... | collective-permute-start | bytes 1179656 | tf_op jit(solution)/shard_map/ppermute | solution.py:197
  62.3 0.0 collective-permute-done.5.refs_4_
  62.3 0.0 collective-permute-done.8.refs_7_
  62.3 0.0 collective-permute-done.7.refs_6_
  62.3 1.6 %collective-permute-done.6.refs_5_ = f32[96,1024]{1,0:T(8,128)S(1)} collective-permute-done((f32[96,1024]{1,0:T(8,128)S(1)}, f32[96,1024]{1,0:T(8,128)S(1)}, u32[]{:S(2)}, u32[]{:S(2)}) %collective-permute-start.6) | collective-permute-done | bytes 393248 | tf_op jit(solution)/shard_map/ppermute | solution.py:197
  63.9 0.5 all-to-all-done.1.parts_ref
  64.4 0.0 copy-done.1
  64.4 2.2 %shard_map.59 = f32[32,4,128]{2,1,0:T(4,128)S(1)} custom-call(f32[8,32,384]{2,1,0:T(8,128)S(1)} %all-to-all-done.1.parts_ref, f32[24,24]{1,0:T(8,128)S(1)} %copy-done.1, f32[96,1024]{1,0:T(8,128)S(1)} %shard_map.58.refs_0_, f32[96,1024]{1,0:T(8,128)S(1)} %collective-permute-done.2.refs_1_, f32[96,1024]{1,0:T(8,128)S(1)} %collective-permute-done.3.refs_2_, ...), custom_call_target="tpu_custom_call" | custom-call | flops 75497472 | bytes 4000000 | tf_op jit(solution)/shard_map/pallas_call | solution.py:184
  66.5 18.6 %all_to_all.20 = f32[32,4,128]{2,1,0:T(4,128)S(1)} all-to-all(f32[32,4,128]{2,1,0:T(4,128)S(1)} %shard_map.59), channel_id=1, replica_groups=mesh['z'=12,'core'=2,'y'=8,'x'=4] {'y','x'}, dimensions={0} | all-to-all | bytes 131072 | tf_op jit(solution)/shard_map/all_to_all | solution.py:220
  85.1 13.1 %all_to_all.21 = f32[32,4,128]{2,1,0:T(4,128)S(1)} all-to-all(f32[32,4,128]{2,1,0:T(4,128)S(1)} %broadcast_in_dim.2), channel_id=1, replica_groups=mesh['z'=12,'core'=2,'y'=8,'x'=4] {'y','x'}, dimensions={0} | all-to-all | bytes 131072 | tf_op jit(solution)/shard_map/all_to_all | solution.py:222
  98.2 0.6 copy.9
  (5 shorter events, 0.1 us)
Async XLA Ops:
  0.0 9.2 %copy-start = (f32[1,32,1024]{2,1,0:T(8,128)S(1)}, f32[1,32,1024]{2,1,0:T(8,128)}, u32[]{:S(2)}) copy-start(f32[1,32,1024]{2,1,0:T(8,128)} %param.9) | copy-start | bytes 393220
  0.0 9.2 %collective-permute-start = (f32[32,1024]{1,0:T(8,128)}, f32[32,1024]{1,0:T(8,128)S(1)}, u32[]{:S(2)}, u32[]{:S(2)}) collective-permute-start(f32[32,1024]{1,0:T(8,128)} %bitcast.6), channel_id=1, source_target_pairs={{0,32},{32,0},{1,33},{33,1},{2,34},{34,2},{3,35},{35,3},{4,36},{36... | collective-permute-start | bytes 393224 | tf_op jit(solution)/shard_map/ppermute | solution.py:197
  9.3 21.3 %collective-permute-start.1 = (f32[64,1024]{1,0:T(8,128)S(1)}, f32[64,1024]{1,0:T(8,128)S(1)}, u32[]{:S(2)}, u32[]{:S(2)}) collective-permute-start(f32[64,1024]{1,0:T(8,128)S(1)} %pad_maximum_fusion), channel_id=1, source_target_pairs={{0,512},{32,288},{64,576},{96,352},{128,640},{160,416},{192,704},{... | collective-permute-start | bytes 786440 | tf_op jit(solution)/shard_map/ppermute | solution.py:211
  19.1 22.6 %all-to-all-start = ((f32[4,256,384]{2,1,0:T(8,128)}), f32[4,256,384]{2,1,0:T(8,128)S(1)}, u32[]{:S(2)}, u32[]{:S(2)}) async-start(f32[4,256,384]{2,1,0:T(8,128)} %shard_map.56), calls=%async_computation | async-start | bytes 3145728 | tf_op jit(solution)/shard_map/all_to_all | solution.py:216
  30.6 33.8 %copy-start.1 = (f32[24,24]{1,0:T(8,128)S(1)}, f32[24,24]{1,0:T(8,128)}, u32[]{:S(2)}) copy-start(f32[24,24]{1,0:T(8,128)} %metric_ref.1) | copy-start | bytes 6916
  30.6 23.6 %collective-permute-start.4 = (f32[96,1024]{1,0:T(8,128)S(1)}, f32[96,1024]{1,0:T(8,128)S(1)}, u32[]{:S(2)}, u32[]{:S(2)}) collective-permute-start(f32[96,1024]{1,0:T(8,128)S(1)} %shard_map.58.refs_0_), channel_id=1, source_target_pairs={{0,128},{64,192},{128,256},{192,320},{256,384},{320,448},{384,512}... | collective-permute-start | bytes 1179656 | tf_op jit(solution)/shard_map/ppermute | solution.py:197
  35.9 20.3 %collective-permute-start.3 = (f32[96,1024]{1,0:T(8,128)S(1)}, f32[96,1024]{1,0:T(8,128)S(1)}, u32[]{:S(2)}, u32[]{:S(2)}) collective-permute-start(f32[96,1024]{1,0:T(8,128)S(1)} %shard_map.58.refs_0_), channel_id=1, source_target_pairs={{0,704},{64,0},{128,64},{192,128},{256,192},{320,256},{384,320},{4... | collective-permute-start | bytes 1179656 | tf_op jit(solution)/shard_map/ppermute | solution.py:197
  37.8 22.5 %collective-permute-start.2 = (f32[96,1024]{1,0:T(8,128)S(1)}, f32[96,1024]{1,0:T(8,128)S(1)}, u32[]{:S(2)}, u32[]{:S(2)}) collective-permute-start(f32[96,1024]{1,0:T(8,128)S(1)} %shard_map.58.refs_0_), channel_id=1, source_target_pairs={{0,64},{64,128},{128,192},{192,256},{256,320},{320,384},{384,448},... | collective-permute-start | bytes 1179656 | tf_op jit(solution)/shard_map/ppermute | solution.py:197
  42.5 21.8 %all-to-all-start.1 = ((f32[8,32,384]{2,1,0:T(8,128)}), f32[8,32,384]{2,1,0:T(8,128)S(1)}, u32[]{:S(2)}, u32[]{:S(2)}) async-start(f32[8,32,384]{2,1,0:T(8,128)} %shard_map.57), calls=%async_computation.1 | async-start | bytes 786432 | tf_op jit(solution)/shard_map/all_to_all | solution.py:218
  51.0 11.4 %collective-permute-start.5 = (f32[96,1024]{1,0:T(8,128)S(1)}, f32[96,1024]{1,0:T(8,128)S(1)}, u32[]{:S(2)}, u32[]{:S(2)}) collective-permute-start(f32[96,1024]{1,0:T(8,128)S(1)} %shard_map.58.refs_0_), channel_id=1, source_target_pairs={{0,32},{32,0},{1,33},{33,1},{2,34},{34,2},{3,35},{35,3},{4,36},{36... | collective-permute-start | bytes 1179656 | tf_op jit(solution)/shard_map/ppermute | solution.py:197
  54.2 8.1 %collective-permute-start.8 = (f32[96,1024]{1,0:T(8,128)S(1)}, f32[96,1024]{1,0:T(8,128)S(1)}, u32[]{:S(2)}, u32[]{:S(2)}) collective-permute-start(f32[96,1024]{1,0:T(8,128)S(1)} %collective-permute-done.4.refs_3_), channel_id=1, source_target_pairs={{0,32},{32,0},{1,33},{33,1},{2,34},{34,2},{3,35},{35,3},{4,36},{36... | collective-permute-start | bytes 1179656 | tf_op jit(solution)/shard_map/ppermute | solution.py:197
  56.2 6.2 %collective-permute-start.7 = (f32[96,1024]{1,0:T(8,128)S(1)}, f32[96,1024]{1,0:T(8,128)S(1)}, u32[]{:S(2)}, u32[]{:S(2)}) collective-permute-start(f32[96,1024]{1,0:T(8,128)S(1)} %collective-permute-done.3.refs_2_), channel_id=1, source_target_pairs={{0,32},{32,0},{1,33},{33,1},{2,34},{34,2},{3,35},{35,3},{4,36},{36... | collective-permute-start | bytes 1179656 | tf_op jit(solution)/shard_map/ppermute | solution.py:197
  60.3 3.6 %collective-permute-start.6 = (f32[96,1024]{1,0:T(8,128)S(1)}, f32[96,1024]{1,0:T(8,128)S(1)}, u32[]{:S(2)}, u32[]{:S(2)}) collective-permute-start(f32[96,1024]{1,0:T(8,128)S(1)} %collective-permute-done.2.refs_1_), channel_id=1, source_target_pairs={{0,32},{32,0},{1,33},{33,1},{2,34},{34,2},{3,35},{35,3},{4,36},{36... | collective-permute-start | bytes 1179656 | tf_op jit(solution)/shard_map/ppermute | solution.py:197
